TPU v7x, 256 devices: a whole 4x4x8 slice. The times are simulated.
256 devices in a mesh: dp: 32 (over y, z), mp: 8 (over x, core).
Axes of the slice: x: 4, y: 4, z: 8, core: 2. Of those that a mesh axis runs over, the one named last changes fastest.
Arguments:
- grads: bfloat16 [512, 512, 512], P('dp', 'mp'), may hold values from -0.25 to 0.25
- old_stat: float32 [512, 512, 512], P('dp', 'mp'), as said below
- counts: int32 [32], replicated, may hold values from 1 to 16, 256 in all
Outputs:
- new_stat: float32 [512, 512, 512], P('dp', 'mp')
- roots: bfloat16 [512, 512, 512], P('dp', 'mp')
Inputs may be any that keep to these rules, and one draw needn't show every extreme that they name: The counts sum to 256, and the largest is exactly 16. `old_stat`: every block is symmetric and positive definite.
All inputs are finite; a program needn't handle non-finite values.
Results may differ from a plain program's by a relative error of at most 0.005.
Values may be sent and summed in bfloat16 or wider, within the bound.
A program may use at most 128 MiB of HBM per device.

v0:
```python
import jax
import jax.numpy as jnp
from jax import lax
from jax.sharding import PartitionSpec as P

ITERS = 5


decay_rate = 0.5


def newton_roots(blocks):
    order_size = blocks.shape[-1]
    identity = jnp.eye(order_size, dtype=jnp.float32)
    frob_norm = jnp.sqrt(jnp.sum(blocks * blocks, axis=(1, 2)) + 1e-06)
    scaling = (2.5 / frob_norm)[:, None, None]
    matrix = scaling * blocks
    approx = scaling**0.25 * identity
    for iteration in range(ITERS):
        factor = (5.0 * identity - matrix) * 0.25
        approx = jnp.einsum("nij,njk->nik", approx, factor, precision=lax.Precision.HIGHEST)
        square = jnp.einsum("nij,njk->nik", factor, factor, precision=lax.Precision.HIGHEST)
        fourth = jnp.einsum("nij,njk->nik", square, square, precision=lax.Precision.HIGHEST)
        matrix = jnp.einsum("nij,njk->nik", fourth, matrix, precision=lax.Precision.HIGHEST)
    return approx.astype(jnp.bfloat16)


def lane_roots(gathered):
    return newton_roots(gathered[0])[None]


def on_device(grads, old_stat, counts):
    owned = old_stat.shape[0]
    row_piece = old_stat.shape[1]
    order_size = old_stat.shape[2]
    dp_count = lax.axis_size("dp")
    mp_count = lax.axis_size("mp")
    dp_index = lax.axis_index("dp")
    partial_value = jnp.einsum("krb,krc->kbc", grads, grads, preferred_element_type=jnp.float32)
    gram_rows = lax.psum_scatter(
        partial_value.astype(jnp.bfloat16), "mp", scatter_dimension=1, tiled=True
    ).astype(jnp.float32)
    slot_ids = jnp.arange(owned, dtype=jnp.int32)
    is_valid = slot_ids < counts[dp_index]
    new_rows = jnp.where(is_valid[:, None, None], decay_rate * old_stat + gram_rows, 0.0)
    starts = jnp.cumsum(counts) - counts
    global_rank = starts[dp_index] + slot_ids
    target = global_rank % dp_count
    owners = jnp.arange(dp_count, dtype=jnp.int32)
    select = (is_valid[None, :] & (target[None, :] == owners[:, None])).astype(jnp.float32)
    outgoing = jnp.einsum("wk,krc->wrc", select, new_rows, precision=lax.Precision.HIGHEST)
    incoming = lax.all_to_all(outgoing, "dp", split_axis=0, concat_axis=0, tiled=True)
    distance = (dp_index - starts) % dp_count
    present = distance < counts
    slot_lane = (starts + distance) // dp_count
    lane_ids = jnp.arange(mp_count, dtype=jnp.int32)
    packing = (present[None, :] & (slot_lane[None, :] == lane_ids[:, None])).astype(jnp.float32)
    packed = jnp.einsum("lo,orc->lrc", packing, incoming, precision=lax.Precision.HIGHEST)
    roots_mine = lane_roots(
        lax.all_to_all(packed[:, None], "mp", split_axis=0, concat_axis=2, tiled=True)
    )
    returned = lax.all_to_all(roots_mine, "mp", split_axis=2, concat_axis=0, tiled=True).reshape(
        mp_count, row_piece, order_size
    )
    unpacked = jnp.einsum(
        "lo,lrc->orc", packing.astype(jnp.bfloat16), returned, preferred_element_type=jnp.float32
    ).astype(jnp.bfloat16)
    arrived = lax.all_to_all(unpacked, "dp", split_axis=0, concat_axis=0, tiled=True)
    root_rows = jnp.einsum(
        "wk,wrc->krc", select.astype(jnp.bfloat16), arrived, preferred_element_type=jnp.float32
    ).astype(jnp.bfloat16)
    return (new_rows, root_rows)


def solution(mesh):
    placed = (P("dp", "mp", None), P("dp", "mp", None), P())
    return jax.shard_map(
        on_device,
        mesh=mesh,
        in_specs=placed,
        out_specs=(P("dp", "mp", None), P("dp", "mp", None)),
        check_vma=False,
    )
```

profile of v0, /device:TPU:32, one launch (start us, length us, event | category | flops | bytes accessed | tf_op | source)
XLA Modules:
  0.0 340.6 jit_solution(14180598388226424114)
XLA Ops:
  7.2 1.2 copy-done
  8.4 5.6 %convolution_convert_fusion = bf16[16,512,512]{2,1,0:T(8,128)(2,1)} fusion(bf16[16,64,512]{2,1,0:T(8,128)(2,1)S(1)} %copy-done), kind=kOutput, calls=%fused_computation | convolution fusion | flops 541065216 | bytes 9437184 | tf_op jit(solution)/shard_map/krb,krc->kbc/dot_general | solution.py:39
  14.0 0.6 copy-done.7
  14.9 0.6 dynamic_slice.6
  15.5 0.6 dynamic_slice.7
  16.1 0.7 and_select_fusion.2
  16.8 0.7 iota_compare_fusion.5
  17.4 54.3 %reduce-scatter.2.cloned.1.call-done = bf16[16,64,512]{2,1,0:T(8,128)(2,1)} async-done(((bf16[16,512,512]{2,1,0:T(8,128)(2,1)}), bf16[16,64,512]{2,1,0:T(8,128)(2,1)}) %reduce-scatter.2.cloned.1.call-update) | async-done | bytes 1048592 | tf_op jit(solution)/shard_map/reduce_scatter | solution.py:40
  71.7 1.7 add_select_fusion
  73.4 1.3 copy-done.3
  74.7 2.9 fusion.4
  77.7 4.4 %copy.23 = f32[32,64,512]{2,1,0:T(8,128)} copy(f32[32,64,512]{2,0,1:T(8,128)S(1)} %fusion.4) | data formatting | bytes 8388608 | tf_op jit(solution)/shard_map/wk,krc->wrc/dot_general | solution.py:51
  82.1 10.5 %all-to-all-start = ((f32[32,64,512]{2,1,0:T(8,128)}), f32[32,64,512]{2,1,0:T(8,128)}, u32[]{:S(2)}, u32[]{:S(2)}) async-start(f32[32,64,512]{2,1,0:T(8,128)} %copy.23), calls=%async_computation.1 | async-start | bytes 8388608 | tf_op jit(solution)/shard_map/all_to_all | solution.py:52
  92.6 94.8 %all-to-all-done = f32[32,64,512]{2,1,0:T(8,128)} async-done(((f32[32,64,512]{2,1,0:T(8,128)}), f32[32,64,512]{2,1,0:T(8,128)}, u32[]{:S(2)}, u32[]{:S(2)}) %all-to-all-start) | async-done | bytes 4194336 | tf_op jit(solution)/shard_map/all_to_all | solution.py:52
  187.4 5.8 %fusion.9 = f32[8,1,64,512]{3,0,2,1:T(8,128)S(1)} fusion(f32[32,64,512]{2,1,0:T(8,128)} %all-to-all-done, s32[32]{0:T(128)S(1)} %and_select_fusion, pred[32]{0:T(512)(128)(4,1)S(1)} %get-tuple-element.12), kind=kOutput, calls=%fused_computation.15 | convolution fusion | flops 100663808 | bytes 5243040 | tf_op jit(solution)/shard_map/lo,orc->lrc/dot_general | solution.py:58
  193.2 1.6 copy.25
  194.8 3.7 %all-to-all-start.1 = ((f32[8,1,64,512]{3,2,1,0:T(8,128)}), f32[8,1,64,512]{3,2,1,0:T(8,128)S(1)}, u32[]{:S(2)}, u32[]{:S(2)}) async-start(f32[8,1,64,512]{3,2,1,0:T(8,128)} %copy.25), calls=%async_computation.2 | async-start | bytes 2097152 | tf_op jit(solution)/shard_map/all_to_all | solution.py:60
  198.5 16.0 %all-to-all-done.1 = f32[8,1,64,512]{3,2,1,0:T(8,128)S(1)} async-done(((f32[8,1,64,512]{3,2,1,0:T(8,128)}), f32[8,1,64,512]{3,2,1,0:T(8,128)S(1)}, u32[]{:S(2)}, u32[]{:S(2)}) %all-to-all-start.1) | async-done | bytes 1048608 | tf_op jit(solution)/shard_map/all_to_all | solution.py:60
  214.4 0.9 multiply_reduce_fusion
  216.0 0.2 subtract_multiply_fusion
  216.2 1.9 fusion.98
  218.1 1.8 fusion.99
  220.0 1.9 fusion.100
  221.8 1.9 fusion.29
  223.7 1.8 fusion.101
  225.6 1.8 fusion.102
  227.4 1.9 fusion.25
  229.4 2.3 fusion.103
  231.6 1.8 fusion.104
  233.5 1.9 fusion.21
  235.4 1.8 fusion.105
  237.3 2.9 fusion.12
  240.2 3.1 fusion.15
  243.3 1.9 fusion.31
  245.2 2.1 fusion.27
  247.4 1.9 fusion.23
  249.3 1.8 fusion.13
  251.1 0.8 copy.46
  252.0 0.5 broadcast.254
  252.5 3.8 %reduce.2 = bf16[512,512]{1,0:T(8,128)(2,1)S(1)} reduce(bf16[512,1,1,512]{3,2,1,0:T(2,128)(2,1)S(1)} %bitcast.58, bf16[]{:T(256)} %broadcast.254), dimensions={1,2}, to_apply=%bitcast.53.reduce_sub_computation | reduce | bytes 1048578
  256.3 0.4 reshape.232
  256.7 12.8 %all_to_all.28 = bf16[8,2,16384]{2,1,0:T(2,128)(2,1)S(1)} all-to-all(bf16[8,2,16384]{2,1,0:T(2,128)(2,1)S(1)} %reshape.232), channel_id=1, replica_groups=mesh['dp'=32,'mp'=8] {'mp'}, dimensions={0} | all-to-all | bytes 1048576 | tf_op jit(solution)/shard_map/all_to_all | solution.py:62
  269.5 0.5 reshape.233
  270.1 0.7 convolution_convert_fusion.1
  270.9 1.2 copy.29
  272.1 58.5 %all_to_all.29 = bf16[32,64,512]{2,1,0:T(8,128)(2,1)S(1)} all-to-all(bf16[32,64,512]{2,1,0:T(8,128)(2,1)S(1)} %copy.29), channel_id=1, replica_groups=mesh['dp'=32,'mp'=8] {'dp'}, dimensions={0} | all-to-all | bytes 4194304 | tf_op jit(solution)/shard_map/all_to_all | solution.py:68
  330.5 1.5 fusion.6
  332.1 1.6 copy.31
  (22 shorter events, 0.5 us)
Async XLA Ops:
  7.2 1.2 copy-start
  7.2 64.6 %reduce-scatter.2.cloned.1.call-start = ((), (), s32[]{:S(2)}) async-start(), calls=%async_computation.5 | async-start | bytes 9437184 | tf_op jit(solution)/shard_map/reduce_scatter | solution.py:40
  14.0 0.7 copy-start.7
  14.0 57.7 %copy-start.6 = (f32[16,64,512]{2,1,0:T(8,128)S(1)}, f32[16,64,512]{2,1,0:T(8,128)}, u32[]{:S(2)}) copy-start(f32[16,64,512]{2,1,0:T(8,128)} %param.4) | copy-start | bytes 6291460
  73.4 1.3 copy-start.3
  82.1 105.3 %all-to-all-start = ((f32[32,64,512]{2,1,0:T(8,128)}), f32[32,64,512]{2,1,0:T(8,128)}, u32[]{:S(2)}, u32[]{:S(2)}) async-start(f32[32,64,512]{2,1,0:T(8,128)} %copy.23), calls=%async_computation.1 | async-start | bytes 8388608 | tf_op jit(solution)/shard_map/all_to_all | solution.py:52
  194.8 19.6 %all-to-all-start.1 = ((f32[8,1,64,512]{3,2,1,0:T(8,128)}), f32[8,1,64,512]{3,2,1,0:T(8,128)S(1)}, u32[]{:S(2)}, u32[]{:S(2)}) async-start(f32[8,1,64,512]{3,2,1,0:T(8,128)} %copy.25), calls=%async_computation.2 | async-start | bytes 2097152 | tf_op jit(solution)/shard_map/all_to_all | solution.py:60
  216.2 3.7 %copy-start.5 = (f32[8,1,64,512]{3,2,0,1:T(8,128)}, f32[8,1,64,512]{3,2,0,1:T(8,128)S(1)}, u32[]{:S(2)}) copy-start(f32[8,1,64,512]{3,2,0,1:T(8,128)S(1)} %get-tuple-element.11) | copy-start | bytes 3145732
  233.5 3.8 %copy-start.1 = (f32[512,512]{1,0:T(8,128)}, f32[512,512]{1,0:T(8,128)S(1)}, u32[]{:S(2)}) copy-start(f32[512,512]{1,0:T(8,128)S(1)} %fusion.104) | copy-start | bytes 3145732
  245.2 2.1 copy-start.2
  247.3 1.9 copy-start.4
Sparse Core Ops, SparseCore 0:
  14.1 57.5 reduce-scatter.1
where the time goes:
time: 347 us; the launch traced here: 341 us
  waiting for transfers between devices  165 us (48%)
  blocking collectives  71.3 us (21%)
  matrix products  51.3 us (15%)
  local copies, waits for them, and re-layouts  15.5 us (4%)
  between operations  15.3 us (4%)
  starting transfers between devices  14.2 us (4%)
  other arithmetic  8.09 us (2%)
    all_to_all x1, waiting for transfers between devices, on_device(): lax.all_to_all(outgoing, 'dp', split_axis=0, concat_axis=0, tiled=True)  94.8 us
    all_to_all x1, blocking collectives, on_device(): lax.all_to_all(unpacked, 'dp', split_axis=0, concat_axis=0, tiled=True)  58.5 us
    reduce_scatter x1, waiting for transfers between devices, on_device(): lax.psum_scatter(partial_value.astype(jnp.bfloat16), 'mp', scatter_dimens...  54.3 us
    all_to_all x1, waiting for transfers between devices, on_device(): lax.all_to_all(packed[:, None], 'mp', split_axis=0, concat_axis=2, tiled=...  16 us
    all_to_all x1, blocking collectives, on_device(): lax.all_to_all(roots_mine, 'mp', split_axis=2, concat_axis=0, tiled=True)  12.8 us
    dot_general x5, matrix products, newton_roots(): jnp.einsum('nij,njk->nik', approx, factor, precision=lax.Precision.HIGHEST)  10.9 us
    all_to_all x1, starting transfers between devices, on_device(): lax.all_to_all(outgoing, 'dp', split_axis=0, concat_axis=0, tiled=True)  10.5 us
    dot_general x4, matrix products, newton_roots(): jnp.einsum('nij,njk->nik', fourth, matrix, precision=lax.Precision.HIGHEST)  8.42 us
  transfers between devices with their start and end apart: 3, of which 3 were waited for; matrix products, arithmetic and copies ran while one was open for 1% of the time, Pallas kernels for 0%

commit v1 on v0

v1 whole, which is shorter than its diff:
```python
import jax
import jax.numpy as jnp
from jax import lax
from jax.experimental import pallas as pl
from jax.experimental.pallas import tpu as pltpu
from jax.sharding import PartitionSpec as P

F32 = jnp.float32
BF16 = jnp.bfloat16
MESH = pl.DeviceIdType.MESH

ITERS = 5
DECAY = 0.5
ORDER = 512
ROWS = 64
OWN = 16
PEERS = 8
PHASES = OWN // PEERS
CHIPS = 4
LANE = 128
PIECES = CHIPS + 1
GRADS, OLD, GRAM, ROOT = range(4)

TAKES = (
    ((0, 4), (2, 5), (2, 3), (1, 3)),
    ((0, 4), (2, 4), (2, 3), (0, 3)),
)
BLOCKS = (
    tuple((0, (q + 2) % 4, q) for q in range(4)) + ((1, 1, 2), (1, 2, 3), (1, 3, 4), (2, 2, 2), (3, 2, 1), (3, 3, 2)),
    tuple((0, (q + 2) % 4, q) for q in range(4)) + ((1, 1, 2), (1, 2, 3), (2, 2, 2), (3, 1, 0), (3, 2, 1), (3, 3, 2)),
)


def dot(a, b):
    return lax.dot_general(a, b, (((1,), (0,)), ((), ())), preferred_element_type=F32)


def dot_rows(a, b):
    return lax.dot_general(a, b, (((0,), (0,)), ((), ())), preferred_element_type=F32)


def tiles(height, width):
    for j in range(ORDER // width):
        for i in range(ORDER // height):
            yield slice(i * height, (i + 1) * height), slice(j * width, (j + 1) * width)


def newton_root(stat, mat, mat16, low, low16, up16, root, root16, out):
    total = jnp.zeros((1, 1), F32)
    for r, c in tiles(256, 512):
        a = stat[r, c]
        total = total + jnp.sum(a * a, keepdims=True)
    scaling = 2.5 / jnp.sqrt(total + 1e-6)
    for r, c in tiles(128, 512):
        m = stat[r, c] * scaling
        mat[r, c] = m
        mat16[r, c] = m.astype(BF16)
        row = lax.broadcasted_iota(jnp.int32, m.shape, 0) + r.start
        column = lax.broadcasted_iota(jnp.int32, m.shape, 1) + c.start
        x = jnp.where(row == column, 1.25, 0.0) - 0.25 * m
        root[r, c] = x
        root16[r, c] = x.astype(BF16)

    def step(_, carry):
        for r, c in tiles(256, 256):
            t = dot(mat16[r, :], mat16[:, c]) * 0.0625 - 0.625 * mat[r, c]
            low[r, c] = t
            low16[r, c] = t.astype(BF16)
        for r, c in tiles(256, 256):
            up16[r, c] = (dot(low16[r, :], low16[:, c]) + 3.125 * low[r, c]).astype(BF16)
        for r, c in tiles(256, 256):
            mat[r, c] = (625.0 / 256.0) * mat[r, c] + dot(up16[r, :], mat16[:, c])
        mat16[...] = mat[...].astype(BF16)
        for r, c in tiles(256, 256):
            root[r, c] = 1.25 * root[r, c] - 0.25 * dot(root16[r, :], mat16[:, c])
        root16[...] = root[...].astype(BF16)
        return carry

    lax.fori_loop(0, ITERS - 1, step, 0)
    quarter = jnp.sqrt(jnp.sqrt(scaling))
    for r, c in tiles(128, 512):
        out[r, c] = (root[r, c] * quarter).astype(BF16)


def kernel(
    grads, old, gram_out, root_out,
    g_in, o_all, o_send, o_in, gram_send, root_send,
    stat, mat, mat16, low, low16, up16, root, root16,
    load_sem, send_sem, recv_sem,
):
    dp = lax.axis_index("dp")
    me = lax.axis_index("mp")
    x, core = me // 2, lax.rem(me, 2)

    loads = [
        pltpu.make_async_copy(old.at[pl.ds(p * PEERS, PEERS)], o_all.at[pl.ds(p * PEERS, PEERS)], load_sem.at[p])
        for p in range(PHASES)
    ]
    for load in loads:
        load.start()

    peers = []
    for dr in range(CHIPS):
        for dc in range(2):
            peers.append((dr, dc, lax.rem(x + CHIPS - dr, CHIPS) * 2 + lax.rem(core + dc, 2)))

    barrier = pltpu.get_barrier_semaphore()
    for _, _, to in peers[1:]:
        pl.semaphore_signal(barrier, inc=1, device_id=(dp, to), device_id_type=MESH)
    pl.semaphore_wait(barrier, PEERS - 1)

    def transfers(kind, p):
        out = []
        for d, (dr, dc, to) in enumerate(peers):
            if kind == GRADS:
                src = grads.at[p * PEERS + to]
                dst = g_in.at[p, pl.ds(pl.multiple_of(me * ROWS, ROWS), ROWS)]
            elif kind == OLD:
                a, b = TAKES[p][dr]
                src = o_send.at[p * PEERS + to, pl.ds(a, b - a)]
                dst = o_in.at[p, dr * 2 + core, pl.ds(a, b - a)]
            elif kind == GRAM:
                src = gram_send.at[p, pl.ds(pl.multiple_of(to * ROWS, ROWS), ROWS)]
                dst = gram_out.at[p * PEERS + me]
            else:
                src = root_send.at[p, pl.ds(pl.multiple_of(to * ROWS, ROWS), ROWS)]
                dst = root_out.at[p * PEERS + me]
            if d == 0:
                out.append(pltpu.make_async_copy(src, dst, recv_sem.at[kind, p, d]))
            else:
                out.append(
                    pltpu.make_async_remote_copy(
                        src_ref=src,
                        dst_ref=dst,
                        send_sem=send_sem.at[kind, p, d],
                        recv_sem=recv_sem.at[kind, p, d],
                        device_id=(dp, to),
                        device_id_type=MESH,
                    )
                )
        return out

    moves = {(kind, p): transfers(kind, p) for kind in range(4) for p in range(PHASES)}

    def start(kind, p):
        for copy in moves[kind, p]:
            copy.start()

    def arrive(kind, p):
        own, *rest = moves[kind, p]
        own.wait()
        for copy in rest:
            copy.wait_recv()

    def stage_old(p):
        loads[p].wait()
        k = slice(p * PEERS, (p + 1) * PEERS)
        for q in range(PIECES):
            columns = pl.ds(pl.multiple_of(lax.rem(x + q + 2, CHIPS) * LANE, LANE), LANE)
            o_send[k, q] = (DECAY * o_all[k, :, columns]).astype(BF16)

    def gram_of(p):
        for r, c in tiles(256, 256):
            part = dot_rows(g_in[p, :, r], g_in[p, :, c])
            stat[r, c] = part
            gram_send[p, r, c] = part.astype(BF16)

    def add_old(p):
        there = [pl.ds(pl.multiple_of(lax.rem(x + r, CHIPS) * LANE, LANE), LANE) for r in range(CHIPS)]
        for r, c, q in BLOCKS[p]:
            block = jnp.concatenate([o_in[p, 2 * r, q], o_in[p, 2 * r + 1, q]], axis=0).astype(F32)
            stat[there[r], there[c]] += block
            if r != c:
                stat[there[c], there[r]] += block.T

    start(GRADS, 0)
    stage_old(0)
    start(OLD, 0)
    stage_old(1)
    arrive(GRADS, 0)
    start(GRADS, 1)
    start(OLD, 1)
    for p in range(PHASES):
        if p:
            arrive(GRADS, p)
        gram_of(p)
        start(GRAM, p)
        arrive(OLD, p)
        add_old(p)
        newton_root(stat, mat, mat16, low, low16, up16, root, root16, root_send.at[p])
        start(ROOT, p)
    for kind in (GRAM, ROOT):
        for p in range(PHASES):
            arrive(kind, p)
    for copies in moves.values():
        for copy in copies[1:]:
            copy.wait_send()


def exchange(grads, old_stat):
    square = (ORDER, ORDER)
    return pl.pallas_call(
        kernel,
        out_shape=[jax.ShapeDtypeStruct((OWN, ROWS, ORDER), BF16)] * 2,
        in_specs=[pl.BlockSpec(memory_space=pl.ANY)] * 2,
        out_specs=[pl.BlockSpec(memory_space=pl.ANY)] * 2,
        scratch_shapes=[
            pltpu.VMEM((PHASES,) + square, BF16),
            pltpu.VMEM((OWN, ROWS, ORDER), F32),
            pltpu.VMEM((OWN, PIECES, ROWS, LANE), BF16),
            pltpu.VMEM((PHASES, PEERS, PIECES, ROWS, LANE), BF16),
            pltpu.VMEM((PHASES,) + square, BF16),
            pltpu.VMEM((PHASES,) + square, BF16),
        ]
        + [pltpu.VMEM(square, d) for d in (F32, F32, BF16, F32, BF16, BF16, F32, BF16)]
        + [
            pltpu.SemaphoreType.DMA((PHASES,)),
            pltpu.SemaphoreType.DMA((4, PHASES, PEERS)),
            pltpu.SemaphoreType.DMA((4, PHASES, PEERS)),
        ],
        compiler_params=pltpu.CompilerParams(
            collective_id=0, has_side_effects=True, vmem_limit_bytes=40 << 20
        ),
        cost_estimate=pl.CostEstimate(flops=36 * 2 * ORDER**3, bytes_accessed=6 << 20, transcendentals=0),
        name="refresh",
    )(grads, old_stat)


def on_device(grads, old_stat, counts):
    gram_rows, root_rows = exchange(grads, old_stat)
    filled = (jnp.arange(OWN, dtype=jnp.int32) < counts[lax.axis_index("dp")])[:, None, None]
    new_rows = jnp.where(filled, DECAY * old_stat + gram_rows.astype(F32), 0.0)
    return new_rows, jnp.where(filled, root_rows, jnp.zeros((), BF16))


def solution(mesh):
    placed = P("dp", "mp", None)
    return jax.shard_map(
        on_device,
        mesh=mesh,
        in_specs=(placed, placed, P()),
        out_specs=(placed, placed),
        check_vma=False,
    )
```

time: 347 us -> 55.9 us (0.16)
  the two profiles are of different devices: /device:TPU:32 before, /device:TPU:1 now
where the time goes in v1:
time: 55.9 us; the launch traced here: 55.8 us
  Pallas kernels  47.5 us (85%)
  local copies, waits for them, and re-layouts  4.05 us (7%)
  other arithmetic  3.53 us (6%)
  between operations  0.66 us (1%)
    pallas_call x1, Pallas kernels, exchange(): pl.pallas_call(kernel, out_shape=[jax.ShapeDtypeStruct((OWN, ROWS, ORDER)...  47.5 us
    unnamed x4, local copies, waits for them, and re-layouts  2.81 us
    select_n x1, other arithmetic, on_device(): new_rows = jnp.where(filled, DECAY * old_stat + gram_rows.astype(F32), 0.0)  1.77 us
    dynamic_slice x1, local copies, waits for them, and re-layouts, on_device(): counts[lax.axis_index('dp')]  1.24 us

profile of v1, /device:TPU:1, one launch (start us, length us, event | category | flops | bytes accessed | tf_op | source)
XLA Modules:
  0.0 55.8 jit_solution(16844039033046826183)
XLA Ops:
  0.6 1.2 %dynamic_slice.3 = s32[1]{0:T(128)} dynamic-slice(s32[32]{0:T(128)} %param.5, s32[]{:T(128)S(6)} %select_n.11), dynamic_slice_sizes={1} | dynamic-slice | bytes 12 | tf_op jit(solution)/shard_map/dynamic_slice | solution.py:231
  1.9 0.6 %iota_compare_fusion = pred[16]{0:T(512)(128)(4,1)S(1)} fusion(s32[]{:T(128)} %bitcast), kind=kLoop, calls=%fused_computation.2 | loop fusion | flops 16 | bytes 20 | tf_op jit(solution)/shard_map/lt | solution.py:231
  2.5 0.0 copy-start
  2.5 1.6 %copy-done = f32[16,64,512]{2,1,0:T(8,128)S(1)} copy-done((f32[16,64,512]{2,1,0:T(8,128)S(1)}, f32[16,64,512]{2,1,0:T(8,128)}, u32[]{:S(2)}) %copy-start) | copy-done | bytes 2097176
  4.1 0.0 copy-start.1
  4.1 1.2 %copy-done.1 = bf16[16,64,512]{2,1,0:T(8,128)(2,1)S(1)} copy-done((bf16[16,64,512]{2,1,0:T(8,128)(2,1)S(1)}, bf16[16,64,512]{2,1,0:T(8,128)(2,1)}, u32[]{:S(2)}) %copy-start.1) | copy-done | bytes 1048600
  5.4 47.5 %refresh.1 = (bf16[16,64,512]{2,1,0:T(8,128)(2,1)S(1)}, bf16[16,64,512]{2,1,0:T(8,128)(2,1)S(1)}) custom-call(bf16[16,64,512]{2,1,0:T(8,128)(2,1)S(1)} %copy-done.1, f32[16,64,512]{2,1,0:T(8,128)S(1)} %copy-done), custom_call_target="tpu_custom_call" | custom-call | flops 9663676416 | bytes 6291456 | tf_op jit(solution)/shard_map/refresh/pallas_call | solution.py:202
  52.9 1.8 %add_select_fusion = f32[16,64,512]{2,1,0:T(8,128)} fusion(bf16[16,64,512]{2,1,0:T(8,128)(2,1)S(1)} %get-tuple-element.4, f32[16,64,512]{2,1,0:T(8,128)S(1)} %copy-done, pred[16]{0:T(512)(128)(4,1)S(1)} %iota_compare_fusion), kind=kLoop, calls=%fused_computation | loop fusion | flops 2097152 | bytes 5242896 | tf_op jit(solution)/shard_map/jit(_where)/select_n | solution.py:232
  54.7 1.1 %broadcast_select_fusion = bf16[16,64,512]{2,1,0:T(8,128)(2,1)} fusion(bf16[16,64,512]{2,1,0:T(8,128)(2,1)S(1)} %get-tuple-element.5, pred[16]{0:T(512)(128)(4,1)S(1)} %iota_compare_fusion), kind=kLoop, calls=%fused_computation.1 | loop fusion | flops 524288 | bytes 2097168 | tf_op jit(solution)/shard_map/jit(_where)/select_n | solution.py:233
Async XLA Ops:
  2.5 1.6 %copy-start = (f32[16,64,512]{2,1,0:T(8,128)S(1)}, f32[16,64,512]{2,1,0:T(8,128)}, u32[]{:S(2)}) copy-start(f32[16,64,512]{2,1,0:T(8,128)} %old.1) | copy-start | bytes 6291460
  4.1 1.2 %copy-start.1 = (bf16[16,64,512]{2,1,0:T(8,128)(2,1)S(1)}, bf16[16,64,512]{2,1,0:T(8,128)(2,1)}, u32[]{:S(2)}) copy-start(bf16[16,64,512]{2,1,0:T(8,128)(2,1)} %grads.1) | copy-start | bytes 3145732

commit v2 on v1

v2 whole, which is shorter than its diff:
```python
import jax
import jax.numpy as jnp
from jax import lax
from jax.experimental import pallas as pl
from jax.experimental.pallas import tpu as pltpu
from jax.sharding import PartitionSpec as P

F32 = jnp.float32
BF16 = jnp.bfloat16
MESH = pl.DeviceIdType.MESH

ITERS = 5
DECAY = 0.5
ORDER = 512
ROWS = 64
OWN = 16
PEERS = 8
PHASES = OWN // PEERS
CHIPS = 4
LANE = 128
PIECES = CHIPS + 1
HALF = ORDER // 2
KINDS = 7
GRADS, OLD, UPPER, ROWS_NEAR, ROWS_FAR, ROOT_NEAR, ROOT_FAR = range(KINDS)

TAKES = (
    ((0, 4), (2, 5), (2, 3), (1, 3)),
    ((0, 4), (2, 4), (2, 3), (0, 3)),
)
BLOCKS = (
    tuple((0, (q + 2) % 4, q) for q in range(4)) + ((1, 1, 2), (1, 2, 3), (1, 3, 4), (2, 2, 2), (3, 2, 1), (3, 3, 2)),
    tuple((0, (q + 2) % 4, q) for q in range(4)) + ((1, 1, 2), (1, 2, 3), (2, 2, 2), (3, 1, 0), (3, 2, 1), (3, 3, 2)),
)


def dot(a, b):
    return lax.dot_general(a, b, (((1,), (0,)), ((), ())), preferred_element_type=F32)


def dot_rows(a, b):
    return lax.dot_general(a, b, (((0,), (0,)), ((), ())), preferred_element_type=F32)


def tiles(height, width):
    for j in range(ORDER // width):
        for i in range(ORDER // height):
            yield slice(i * height, (i + 1) * height), slice(j * width, (j + 1) * width)


def newton_roots(jobs, work):
    jobs = [job + tuple(ref.at[i] for ref in work) for i, job in enumerate(jobs)]
    scalings = []
    for stat, keep, here, there, out, mat, mat16, low, low16, up16, root, root16 in jobs:
        total = jnp.zeros((1, 1), F32)
        for r, c in tiles(256, 512):
            a = stat[r, c].astype(F32)
            total = total + jnp.sum(a * a, keepdims=True)
        scaling = 2.5 / jnp.sqrt(total + 1e-6)
        scalings.append(scaling)
        for r, c in tiles(128, 512):
            m = stat[r, c].astype(F32) * scaling
            mat[r, c] = m
            mat16[r, c] = m.astype(BF16)
        for i, chip in enumerate((here, there)):
            m = mat[pl.ds(pl.multiple_of(chip * LANE, LANE), LANE), :]
            row = lax.broadcasted_iota(jnp.int32, m.shape, 0) + chip * LANE
            column = lax.broadcasted_iota(jnp.int32, m.shape, 1)
            x = jnp.where(row == column, 1.25, 0.0) - 0.25 * m
            root[i * LANE : (i + 1) * LANE, :] = x
            root16[i * LANE : (i + 1) * LANE, :] = x.astype(BF16)

    first, second = slice(0, HALF), slice(HALF, ORDER)
    upper = ((first, first), (first, second), (second, second))

    def put(ref, r, c, value):
        value = value.astype(BF16)
        ref[r, c] = value
        if r != c:
            ref[c, r] = value.T

    def factors():
        for *_, mat, mat16, low, low16, up16, root, root16 in jobs:
            for r, c in upper:
                t = dot(mat16[r, :], mat16[:, c]) * 0.0625 - 0.625 * mat[r, c]
                low[r, c] = t
                put(low16, r, c, t)
        for *_, mat, mat16, low, low16, up16, root, root16 in jobs:
            for r, c in upper:
                put(up16, r, c, dot(low16[r, :], low16[:, c]) + 3.125 * low[r, c])

    def step(_, carry):
        factors()
        for *_, mat, mat16, low, low16, up16, root, root16 in jobs:
            for r, c in upper:
                mat[r, c] = (625.0 / 256.0) * mat[r, c] + dot(up16[r, :], mat16[:, c])
            for r, c in upper:
                put(mat16, r, c, mat[r, c])
        for *_, mat, mat16, low, low16, up16, root, root16 in jobs:
            for c in (first, second):
                root[:, c] = 1.25 * root[:, c] - 0.25 * dot(root16[...], mat16[:, c])
            root16[...] = root[...].astype(BF16)
        return carry

    lax.fori_loop(0, ITERS - 2, step, 0, unroll=True)
    factors()
    for *_, mat, mat16, low, low16, up16, root, root16 in jobs:
        for c in (first, second):
            low16[first, c] = ((625.0 / 256.0) * root[:, c] + dot(root16[...], up16[:, c])).astype(BF16)
    for scaling, (stat, keep, here, there, out, mat, mat16, low, low16, up16, root, root16) in zip(scalings, jobs):
        quarter = jnp.where(keep, jnp.sqrt(jnp.sqrt(scaling)), 0.0)
        for c in (first, second):
            out[:, c] = ((1.25 * root[:, c] - 0.25 * dot(low16[first, :], mat16[:, c])) * quarter).astype(BF16)


def kernel(
    counts, grads, old, new_out, root_out,
    g_in, o_all, o_send, o_in, stat, full, upper_in, rows_in, new, root_send,
    mat, mat16, low, low16, up16, root, root16,
    load_sem, store_sem, send_sem, recv_sem,
):
    dp = lax.axis_index("dp")
    me = lax.axis_index("mp")
    x, core = me // 2, lax.rem(me, 2)
    turn = 1 - 2 * core
    ahead, behind = lax.rem(x + turn + CHIPS, CHIPS), lax.rem(x - turn + CHIPS, CHIPS)
    served = behind * 2 + core

    filled = counts[dp]
    loads = [
        pltpu.make_async_copy(old.at[pl.ds(p * PEERS, PEERS)], o_all.at[pl.ds(p * PEERS, PEERS)], load_sem.at[p])
        for p in range(PHASES)
    ]
    for load in loads:
        load.start()

    peers = []
    for dr in range(CHIPS):
        for dc in range(2):
            peers.append((dr, dc, lax.rem(x + CHIPS - dr, CHIPS) * 2 + lax.rem(core + dc, 2)))

    barrier = pltpu.get_barrier_semaphore()
    for _, _, to in peers[1:]:
        pl.semaphore_signal(barrier, inc=1, device_id=(dp, to), device_id_type=MESH)
    pl.semaphore_wait(barrier, PEERS - 1)

    moves = {}

    def add(kind, p, src, dst, to):
        copies = moves.setdefault((kind, p), [])
        i = len(copies)
        if to is None:
            copies.append((True, pltpu.make_async_copy(src, dst, recv_sem.at[kind, p, i])))
        else:
            copy = pltpu.make_async_remote_copy(
                src_ref=src,
                dst_ref=dst,
                send_sem=send_sem.at[kind, p, i],
                recv_sem=recv_sem.at[kind, p, i],
                device_id=(dp, to),
                device_id_type=MESH,
            )
            copies.append((False, copy))

    def rows(device):
        return pl.ds(pl.multiple_of(device * ROWS, ROWS), ROWS)

    for p in range(PHASES):
        for d, (dr, dc, to) in enumerate(peers):
            target = to if d else None
            a, b = TAKES[p][dr]
            add(GRADS, p, grads.at[p * PEERS + to], g_in.at[p, rows(me)], target)
            add(OLD, p, o_send.at[p * PEERS + to, pl.ds(a, b - a)], o_in.at[p, dr * 2 + core, pl.ds(a, b - a)], target)
        for i in range(CHIPS):
            part = (p, slice(i * LANE, (i + 1) * LANE), slice(i * LANE, ORDER))
            add(UPPER, p, full.at[part], upper_in.at[part], ahead * 2 + core)
        for far, chip, block, k in ((0, behind, full, p * PEERS + me), (1, ahead, upper_in, p * PEERS + served)):
            targets = ((me, None, core), (x * 2 + 1 - core,) * 2 + (1 - core,))
            targets += ((chip * 2 + core,) * 2 + (2 + core,), (chip * 2 + 1 - core,) * 2 + (3 - core,))
            for device, target, piece in targets:
                add(ROWS_NEAR + far, p, block.at[p, rows(device)], rows_in.at[k], target)
                add(ROOT_NEAR + far, p, root_send.at[far, p, rows(piece)], root_out.at[k], target)

    def start(kind, p):
        for _, copy in moves[kind, p]:
            copy.start()

    def arrive(kind, p):
        for local, copy in moves[kind, p]:
            if local:
                copy.wait()
            else:
                copy.wait_recv()

    def stage_old(p):
        loads[p].wait()
        k = slice(p * PEERS, (p + 1) * PEERS)
        for q in range(PIECES):
            columns = pl.ds(pl.multiple_of(lax.rem(x + q + 2, CHIPS) * LANE, LANE), LANE)
            o_send[k, q] = (DECAY * o_all[k, :, columns]).astype(BF16)

    def gram_of(p):
        for r, c in tiles(256, 256):
            stat[p, r, c] = dot_rows(g_in[p, :, r], g_in[p, :, c])

    def add_old(p):
        there = [pl.ds(pl.multiple_of(lax.rem(x + r, CHIPS) * LANE, LANE), LANE) for r in range(CHIPS)]
        for r, c, q in BLOCKS[p]:
            block = jnp.concatenate([o_in[p, 2 * r, q], o_in[p, 2 * r + 1, q]], axis=0).astype(F32)
            stat[p, there[r], there[c]] += block
            if r != c:
                stat[p, there[c], there[r]] += block.T
        full[p] = stat[p].astype(BF16)

    work = (mat, mat16, low, low16, up16, root, root16)

    def near(p):
        return stat.at[p], p * PEERS + me < filled, x, behind, root_send.at[0, p]

    def far(p):
        return upper_in.at[p], p * PEERS + served < filled, x, ahead, root_send.at[1, p]

    def mirror(p):
        arrive(UPPER, p)
        for r in range(CHIPS):
            for c in range(r + 1, CHIPS):
                a, b = slice(r * LANE, (r + 1) * LANE), slice(c * LANE, (c + 1) * LANE)
                upper_in[p, b, a] = upper_in[p, a, b].T
        start(ROWS_FAR, p)

    stores = [
        pltpu.make_async_copy(new.at[pl.ds(p * PEERS, PEERS)], new_out.at[pl.ds(p * PEERS, PEERS)], store_sem.at[p])
        for p in range(PHASES)
    ]

    def refresh_rows(p):
        arrive(ROWS_NEAR, p)
        arrive(ROWS_FAR, p)
        for k in range(p * PEERS, (p + 1) * PEERS):
            decayed = DECAY * o_all[k]
            rest = decayed - decayed.astype(BF16).astype(F32)
            new[k] = jnp.where(k < filled, rows_in[k].astype(F32) + rest, 0.0)
        stores[p].start()

    start(GRADS, 0)
    stage_old(0)
    start(OLD, 0)
    stage_old(1)
    arrive(GRADS, 0)
    start(GRADS, 1)
    gram_of(0)
    arrive(OLD, 0)
    start(OLD, 1)
    add_old(0)
    newton_roots([near(0)], work)
    start(UPPER, 0)
    arrive(GRADS, 1)
    gram_of(1)
    arrive(OLD, 1)
    add_old(1)
    start(UPPER, 1)
    newton_roots([near(1)], work)
    mirror(0)
    start(ROWS_NEAR, 0)
    start(ROOT_NEAR, 0)
    newton_roots([far(0)], work)
    start(ROOT_FAR, 0)
    mirror(1)
    start(ROWS_NEAR, 1)
    start(ROOT_NEAR, 1)
    refresh_rows(0)
    newton_roots([far(1)], work)
    start(ROOT_FAR, 1)
    refresh_rows(1)
    for p in range(PHASES):
        arrive(ROOT_NEAR, p)
        arrive(ROOT_FAR, p)
        stores[p].wait()
    for copies in moves.values():
        for local, copy in copies:
            if not local:
                copy.wait_send()


def exchange(counts, grads, old_stat):
    square = (ORDER, ORDER)
    half = (HALF, ORDER)
    return pl.pallas_call(
        kernel,
        out_shape=[jax.ShapeDtypeStruct((OWN, ROWS, ORDER), d) for d in (F32, BF16)],
        in_specs=[pl.BlockSpec(memory_space=pltpu.SMEM)] + [pl.BlockSpec(memory_space=pltpu.HBM)] * 2,
        out_specs=[pl.BlockSpec(memory_space=pl.ANY)] * 2,
        scratch_shapes=[
            pltpu.VMEM((PHASES,) + square, BF16),
            pltpu.VMEM((OWN, ROWS, ORDER), F32),
            pltpu.VMEM((OWN, PIECES, ROWS, LANE), BF16),
            pltpu.VMEM((PHASES, PEERS, PIECES, ROWS, LANE), BF16),
            pltpu.VMEM((PHASES,) + square, F32),
            pltpu.VMEM((PHASES,) + square, BF16),
            pltpu.VMEM((PHASES,) + square, BF16),
            pltpu.VMEM((OWN, ROWS, ORDER), BF16),
            pltpu.VMEM((OWN, ROWS, ORDER), F32),
            pltpu.VMEM((2, PHASES) + half, BF16),
        ]
        + [pltpu.VMEM((2,) + square, d) for d in (F32, BF16, F32, BF16, BF16)]
        + [pltpu.VMEM((2,) + half, d) for d in (F32, BF16)]
        + [
            pltpu.SemaphoreType.DMA((PHASES,)),
            pltpu.SemaphoreType.DMA((PHASES,)),
            pltpu.SemaphoreType.DMA((KINDS, PHASES, PEERS)),
            pltpu.SemaphoreType.DMA((KINDS, PHASES, PEERS)),
        ],
        compiler_params=pltpu.CompilerParams(
            collective_id=0, has_side_effects=True, vmem_limit_bytes=61 << 20
        ),
        cost_estimate=pl.CostEstimate(flops=60 * 2 * ORDER**3, bytes_accessed=6 << 20, transcendentals=0),
        name="refresh",
    )(counts, grads, old_stat)


def copy_out_kernel(new, root, new_out, root_out, new_held, root_held, load_sem, store_sem):
    loads, stores = [], []
    for i in range(CUTS):
        part = pl.ds(i * (OWN // CUTS), OWN // CUTS)
        for a, (src, held, dst) in enumerate(((new, new_held, new_out), (root, root_held, root_out))):
            loads.append(pltpu.make_async_copy(src.at[part], held.at[part], load_sem.at[a, i]))
            stores.append(pltpu.make_async_copy(held.at[part], dst.at[part], store_sem.at[a, i]))
    for load in loads:
        load.start()
    for load, store in zip(loads, stores):
        load.wait()
        store.start()
    for store in stores:
        store.wait()


CUTS = 4


def copy_out(new, root):
    return pl.pallas_call(
        copy_out_kernel,
        out_shape=[jax.ShapeDtypeStruct(a.shape, a.dtype) for a in (new, root)],
        in_specs=[pl.BlockSpec(memory_space=pl.ANY)] * 2,
        out_specs=[pl.BlockSpec(memory_space=pltpu.HBM)] * 2,
        scratch_shapes=[pltpu.VMEM(a.shape, a.dtype) for a in (new, root)]
        + [pltpu.SemaphoreType.DMA((2, CUTS))] * 2,
        compiler_params=pltpu.CompilerParams(vmem_limit_bytes=61 << 20),
        name="copy_out",
    )(new, root)


def on_device(grads, old_stat, counts):
    return copy_out(*exchange(counts, grads, old_stat))


def solution(mesh):
    placed = P("dp", "mp", None)
    return jax.shard_map(
        on_device,
        mesh=mesh,
        in_specs=(placed, placed, P()),
        out_specs=(placed, placed),
        check_vma=False,
    )
```

time: 55.9 us -> 49.8 us (0.89)
  local copies, waits for them, and re-layouts: 4.05 us -> 0 us
  other arithmetic: 3.53 us -> 0 us
  Pallas kernels: 47.5 us -> 48.9 us
    select_n x2 -> x0, other arithmetic: 2.88 us -> none  [the longest x1 1.77 us: on_device(): new_rows = jnp.where(filled, DECAY * old_stat + gram_rows.astype(F32), 0.0)]
    pallas_call x0 -> x1, Pallas kernels: none -> 2.83 us  [copy_out(): pl.pallas_call(copy_out_kernel, out_shape=[jax.ShapeDtypeStruct(a.shape,...]
    unnamed x4 -> x0, local copies, waits for them, and re-layouts: 2.81 us -> none
    pallas_call x1, Pallas kernels: 47.5 us -> 46 us  [exchange(): pl.pallas_call(kernel, out_shape=[jax.ShapeDtypeStruct((OWN, ROWS, ORDER)...]
    dynamic_slice x1 -> x0, local copies, waits for them, and re-layouts: 1.24 us -> none  [on_device(): counts[lax.axis_index('dp')]]
    lt x1 -> x0, other arithmetic: 0.65 us -> none  [on_device(): jnp.arange(OWN, dtype=jnp.int32) < counts[lax.axis_index('dp')]]
where the time goes in v2:
time: 49.8 us; the launch traced here: 49.7 us
  Pallas kernels  48.9 us (98%)
  between operations  0.8 us (2%)
    pallas_call x1, Pallas kernels, exchange(): pl.pallas_call(kernel, out_shape=[jax.ShapeDtypeStruct((OWN, ROWS, ORDER)...  46 us
    pallas_call x1, Pallas kernels, copy_out(): pl.pallas_call(copy_out_kernel, out_shape=[jax.ShapeDtypeStruct(a.shape,...  2.83 us

profile of v2, /device:TPU:1, one launch (start us, length us, event | category | flops | bytes accessed | tf_op | source)
XLA Modules:
  0.0 49.7 jit_solution(6160299118784607871)
XLA Ops:
  0.6 46.0 %refresh.1 = (f32[16,64,512]{2,1,0:T(8,128)}, bf16[16,64,512]{2,1,0:T(8,128)(2,1)}) custom-call(s32[32]{0:T(128)} %counts.1, bf16[16,64,512]{2,1,0:T(8,128)(2,1)} %grads.1, f32[16,64,512]{2,1,0:T(8,128)} %old.1), custom_call_target="tpu_custom_call" | custom-call | flops 16106127360 | bytes 6291456 | tf_op jit(solution)/shard_map/refresh/pallas_call | solution.py:287
  46.7 2.8 %copy_out.1 = (f32[16,64,512]{2,1,0:T(8,128)}, bf16[16,64,512]{2,1,0:T(8,128)(2,1)}) custom-call(f32[16,64,512]{2,1,0:T(8,128)} %get-tuple-element.4.new, bf16[16,64,512]{2,1,0:T(8,128)(2,1)} %get-tuple-element.5.root), custom_call_target="tpu_custom_call" | custom-call | tf_op jit(solution)/shard_map/copy_out/pallas_call | solution.py:340

commit v3 on v2

--- a/solution.py
+++ b/solution.py
@@ -262,14 +262,14 @@
     mirror(0)
     start(ROWS_NEAR, 0)
     start(ROOT_NEAR, 0)
+    start(ROWS_NEAR, 1)
+    start(ROOT_NEAR, 1)
     newton_roots([far(0)], work)
     start(ROOT_FAR, 0)
     mirror(1)
-    start(ROWS_NEAR, 1)
-    start(ROOT_NEAR, 1)
-    refresh_rows(0)
     newton_roots([far(1)], work)
     start(ROOT_FAR, 1)
+    refresh_rows(0)
     refresh_rows(1)
     for p in range(PHASES):
         arrive(ROOT_NEAR, p)

time: 49.8 us -> 49.2 us (0.988)
  Pallas kernels: 48.9 us -> 48.2 us
    pallas_call x1, Pallas kernels: 46 us -> 45.4 us  [exchange(): pl.pallas_call(kernel, out_shape=[jax.ShapeDtypeStruct((OWN, ROWS, ORDER)...]
where the time goes in v3:
time: 49.2 us; the launch traced here: 49 us
  Pallas kernels  48.2 us (98%)
  between operations  0.8 us (2%)
    pallas_call x1, Pallas kernels, exchange(): pl.pallas_call(kernel, out_shape=[jax.ShapeDtypeStruct((OWN, ROWS, ORDER)...  45.4 us
    pallas_call x1, Pallas kernels, copy_out(): pl.pallas_call(copy_out_kernel, out_shape=[jax.ShapeDtypeStruct(a.shape,...  2.83 us

profile of v3, /device:TPU:1, one launch (start us, length us, event | category | flops | bytes accessed | tf_op | source)
XLA Modules:
  0.0 49.0 jit_solution(15814634262820958767)
XLA Ops:
  0.6 45.4 %refresh.1 = (f32[16,64,512]{2,1,0:T(8,128)}, bf16[16,64,512]{2,1,0:T(8,128)(2,1)}) custom-call(s32[32]{0:T(128)} %counts.1, bf16[16,64,512]{2,1,0:T(8,128)(2,1)} %grads.1, f32[16,64,512]{2,1,0:T(8,128)} %old.1), custom_call_target="tpu_custom_call" | custom-call | flops 16106127360 | bytes 6291456 | tf_op jit(solution)/shard_map/refresh/pallas_call | solution.py:287
  46.1 2.8 %copy_out.1 = (f32[16,64,512]{2,1,0:T(8,128)}, bf16[16,64,512]{2,1,0:T(8,128)(2,1)}) custom-call(f32[16,64,512]{2,1,0:T(8,128)} %get-tuple-element.4.new, bf16[16,64,512]{2,1,0:T(8,128)(2,1)} %get-tuple-element.5.root), custom_call_target="tpu_custom_call" | custom-call | tf_op jit(solution)/shard_map/copy_out/pallas_call | solution.py:340
